TPU v7x, 32 devices: a whole 2x2x4 slice. The times are simulated.
32 devices in a mesh: section: 2 (over core), seq: 4 (over y, x), dp: 4 (over z).
Axes of the slice: x: 2, y: 2, z: 4, core: 2. Of those that a mesh axis runs over, the one named last changes fastest.
Arguments:
- section_input: bfloat16 [2, 4, 512, 4096], P('section', 'dp', 'seq'), may hold values from -6 to 6
- saved_qkv: bfloat16 [2, 4, 512, 3, 2048], P('section', 'dp', None, None, 'seq'), may hold values from -14 to 14
- modulation: float32 [2, 4, 2, 4096], P('section', 'dp'), may hold values from -4 to 4
- w_qkv: bfloat16 [2, 4096, 3, 2048], P('section', 'dp', None, 'seq'), may hold values from -0.09375 to 0.09375
- w_out: bfloat16 [2, 2048, 4096], P('section', 'seq'), may hold values from -0.125 to 0.125
- lengths: int32 [4], P('dp'), may hold values from 1 to 512, 1280 in all
- student_out: bfloat16 [4, 512, 4096], P('dp', 'seq'), may hold values from -6 to 6
- teacher_target: bfloat16 [4, 512, 4096], P('dp', 'seq'), may hold values from -6 to 6
Outputs:
- grad_input: bfloat16 [2, 4, 512, 4096], P('section', 'dp', 'seq')
- grad_out: bfloat16 [2, 2048, 4096], P('section', 'seq', 'dp')
Inputs may be any that keep to these rules, and one draw needn't show every extreme that they name: `lengths`: at least one micro-batch is 512 tokens long.
All inputs are finite; a program needn't handle non-finite values. No bound on the sum of `lengths` on one device may be relied on, other than what follows from the above.
Results may differ from a plain program's by a relative error of at most 0.014.
Values may be sent and summed in bfloat16 or wider, within the bound.
No kernel may reach another device: no remote copies, remote signals or barrier semaphores. Data moves between devices by JAX's collectives and lax.ppermute only.
A program may use at most 192 MiB of HBM per device.

v0:
```python
import math

import jax
import jax.numpy as jnp
from jax import lax
from jax.sharding import PartitionSpec as P

HEAD_DIM = 128


def shifted(value, axis, steps):
    count = lax.axis_size(axis)
    initial, last = (max(0, -steps), min(count, count - steps))
    return lax.ppermute(value, axis, [(source, source + steps) for source in range(initial, last)])


def widen(tensor):
    return lax.optimization_barrier(tensor).astype(jnp.float32)


def contract_rows(left_side, right_side):
    return lax.dot_general(
        left_side, right_side, (((0,), (0,)), ((), ())), preferred_element_type=jnp.float32
    )


def layer_norm_parts(tokens):
    values = tokens.astype(jnp.float32)
    center = values - jnp.mean(values, axis=-1, keepdims=True)
    variance = jnp.mean(center * center, axis=-1, keepdims=True)
    inverse = lax.rsqrt(variance + 1e-06)
    return (center * inverse, inverse)


def attend_backward(saved_rows, d_attn, live_keys, head_size):
    row_total = saved_rows.shape[0]
    feature_width = saved_rows.shape[2]
    head_count = feature_width // head_size
    queries = saved_rows[:, 0].reshape(row_total, head_count, head_size).astype(jnp.float32)
    key_rows = saved_rows[:, 1].reshape(row_total, head_count, head_size).astype(jnp.float32)
    value_rows = saved_rows[:, 2].reshape(row_total, head_count, head_size).astype(jnp.float32)
    factor = 1.0 / math.sqrt(head_size)
    scores = jnp.einsum("qhd,khd->hqk", queries, key_rows) * factor
    scores = jnp.where(live_keys[None, None, :], scores, -1e30)
    peak_score = jnp.max(scores, axis=-1, keepdims=True)
    weights = jnp.exp(scores - peak_score)
    weights = weights / jnp.sum(weights, axis=-1, keepdims=True)
    rounded = widen(weights.astype(jnp.bfloat16))
    attn_mixed = jnp.einsum("hqk,khd->qhd", rounded, value_rows).astype(jnp.bfloat16)
    upstream = d_attn.reshape(row_total, head_count, head_size).astype(jnp.float32)
    d_weights = jnp.einsum("qhd,khd->hqk", upstream, value_rows)
    delta_rows = jnp.einsum("qhd,qhd->hq", upstream, widen(attn_mixed))
    d_scores = widen((weights * (d_weights - delta_rows[:, :, None]) * factor).astype(jnp.bfloat16))
    grad_q = jnp.einsum("hqk,khd->qhd", d_scores, key_rows).astype(jnp.bfloat16)
    grad_k = jnp.einsum("hqk,qhd->khd", d_scores, queries).astype(jnp.bfloat16)
    grad_v = jnp.einsum("hqk,qhd->khd", rounded, upstream).astype(jnp.bfloat16)
    stacked = jnp.stack([grad_q, grad_k, grad_v], axis=1).reshape(row_total, 3, feature_width)
    return (attn_mixed.reshape(row_total, feature_width), stacked)


def body(section_input, saved_qkv, modulation, w_qkv, w_out, lengths, student_out, teacher_target):
    section_total = lax.axis_size("section")
    section_pos = lax.axis_index("section")
    seq_pos = lax.axis_index("seq")
    micro_count = section_input.shape[1]
    shard_rows = section_input.shape[2]
    model_width = section_input.shape[3]
    capacity = saved_qkv.shape[2]
    local_width = saved_qkv.shape[4]
    inputs = section_input[0]
    saved_all = saved_qkv[0]
    mods = modulation[0]
    weight_rows = lax.all_gather(w_qkv[0], "dp", axis=0, tiled=True)
    weight_flat = weight_rows.reshape(model_width, 3 * local_width)
    weight_out = w_out[0]
    normed_all, inverse_all = layer_norm_parts(inputs)
    positions = seq_pos * shard_rows + jnp.arange(shard_rows, dtype=jnp.int32)
    row_live = positions[None, :] < lengths[:, None]
    gap = student_out.astype(jnp.float32) - teacher_target.astype(jnp.float32)
    loss_grad = jnp.where(row_live[:, :, None], gap, 0.0).astype(jnp.bfloat16)
    key_positions = jnp.arange(capacity, dtype=jnp.int32)

    def attend_live(saved_rows, d_attn, live_keys):
        attn_mixed, d_saved = attend_backward(saved_rows, d_attn, live_keys, HEAD_DIM)
        return (attn_mixed, d_saved.reshape(capacity, 3 * local_width))

    def section_work(d_output, slot_index, is_live):
        mod_rows = lax.dynamic_index_in_dim(mods, slot_index, 0, False)
        scale_term = mod_rows[0]
        gate_term = mod_rows[1]
        d_branch = (gate_term * d_output.astype(jnp.float32)).astype(jnp.bfloat16)
        d_branch = jnp.where(is_live, d_branch, jnp.zeros_like(d_branch))
        branch_full = lax.all_gather(d_branch, "seq", axis=0, tiled=True)
        live_length = lengths[slot_index]
        live_keys = key_positions < live_length
        saved_rows = lax.dynamic_index_in_dim(saved_all, slot_index, 0, False)

        def attend_branch(branch_rows):
            d_attn = jnp.dot(branch_rows, weight_out.T, preferred_element_type=jnp.float32).astype(
                jnp.bfloat16
            )
            return attend_live(saved_rows, d_attn, live_keys)

        def attend_none(branch_rows):
            return (
                jnp.zeros((capacity, local_width), jnp.bfloat16),
                jnp.zeros((capacity, 3 * local_width), jnp.bfloat16),
            )

        attn_mixed, flat_grads = lax.cond(is_live, attend_branch, attend_none, branch_full)
        d_mod = lax.psum_scatter(
            lax.cond(
                is_live,
                lambda start_row: jnp.dot(
                    flat_grads, weight_flat.T, preferred_element_type=jnp.float32
                ),
                lambda start_row: jnp.zeros(
                    (shard_rows * lax.axis_size("seq"), model_width), jnp.float32
                ),
                jnp.int32(0),
            ),
            "seq",
            scatter_dimension=0,
            tiled=True,
        )
        normed = lax.dynamic_index_in_dim(normed_all, slot_index, 0, False)
        inverse = lax.dynamic_index_in_dim(inverse_all, slot_index, 0, False)
        d_norm = d_mod * (1.0 + scale_term)
        d_layer = inverse * (
            d_norm
            - jnp.mean(d_norm, axis=-1, keepdims=True)
            - normed * jnp.mean(d_norm * normed, axis=-1, keepdims=True)
        )
        d_input = (d_output.astype(jnp.float32) + d_layer).astype(jnp.bfloat16)
        d_input = jnp.where(is_live, d_input, jnp.zeros_like(d_input))
        return (d_input, attn_mixed, branch_full)

    def put_slot(store, fresh, slot_index, is_live):
        older = lax.dynamic_index_in_dim(store, slot_index, 0, False)
        return lax.dynamic_update_index_in_dim(
            store, jnp.where(is_live, fresh, older), slot_index, 0
        )

    def tick(tick_num, carry):
        incoming, grads_in, mixed_store, branch_store = carry
        slot_raw = tick_num - (section_total - 1 - section_pos)
        is_live = jnp.logical_and(slot_raw >= 0, slot_raw < micro_count)
        slot_index = jnp.clip(slot_raw, 0, micro_count - 1)
        last_grad = lax.dynamic_index_in_dim(loss_grad, slot_index, 0, False)
        d_output = jnp.where(section_pos == section_total - 1, last_grad, incoming)
        d_input, attn_mixed, branch_full = section_work(d_output, slot_index, is_live)
        grads_in = put_slot(grads_in, d_input, slot_index, is_live)
        mixed_store = put_slot(mixed_store, attn_mixed, slot_index, is_live)
        branch_store = put_slot(branch_store, branch_full, slot_index, is_live)
        incoming = shifted(d_input, "section", -1)
        return (incoming, grads_in, mixed_store, branch_store)

    start_carry = (
        jnp.zeros((shard_rows, model_width), jnp.bfloat16),
        jnp.zeros((micro_count, shard_rows, model_width), jnp.bfloat16),
        jnp.zeros((micro_count, capacity, local_width), jnp.bfloat16),
        jnp.zeros((micro_count, capacity, model_width), jnp.bfloat16),
    )
    final_carry = lax.fori_loop(0, section_total + micro_count - 1, tick, start_carry)
    grads_in = final_carry[1]
    mixed_store = final_carry[2]
    branch_store = final_carry[3]
    out_local = contract_rows(
        mixed_store.reshape(micro_count * capacity, local_width),
        branch_store.reshape(micro_count * capacity, model_width),
    )
    out_slice = lax.psum_scatter(out_local, "dp", scatter_dimension=1, tiled=True)
    grad_input = grads_in[None]
    grad_out = out_slice.astype(jnp.bfloat16)[None]
    return (grad_input, grad_out)


def solution(mesh):
    in_specs = (
        P("section", "dp", "seq", None),
        P("section", "dp", None, None, "seq"),
        P("section", "dp", None, None),
        P("section", "dp", None, "seq"),
        P("section", "seq", None),
        P("dp"),
        P("dp", "seq", None),
        P("dp", "seq", None),
    )
    out_specs = (P("section", "dp", "seq", None), P("section", "seq", "dp"))
    return jax.shard_map(body, mesh=mesh, in_specs=in_specs, out_specs=out_specs, check_vma=False)
```

profile of v0, /device:TPU:0, one launch (start us, length us, event | category | flops | bytes accessed | tf_op | source)
XLA Modules:
  0.0 786.9 jit_solution(10957422643902414525)
XLA Ops:
  7.2 4.7 copy.33
  18.4 214.6 %all-gather.4.cloned.1.call-done = bf16[1,4096,3,512]{1,3,2,0:T(8,128)(2,1)} async-done(((bf16[1,1024,3,512]{1,3,2,0:T(8,128)(2,1)}), bf16[1,4096,3,512]{1,3,2,0:T(8,128)(2,1)}) %all-gather.4.cloned.1.call-update) | async-done | bytes 12582928 | tf_op jit(solution)/shard_map/all_gather | solution.py:73
  233.0 16.6 %copy.34 = bf16[4096,1536]{1,0:T(8,128)(2,1)} copy(bf16[4096,1536]{0,1:T(8,128)(2,1)} %bitcast.145) | data formatting | bytes 25165824
  252.6 2.5 broadcast_in_dim.89
  255.1 369.7 %while.22 = (s32[]{:T(128)}, bf16[128,4096]{1,0:T(8,128)(2,1)}, bf16[1,128,4096]{2,1,0:T(8,128)(2,1)}, bf16[1,512,512]{1,2,0:T(8,128)(2,1)}, bf16[1,512,4096]{2,...) while((s32[]{:T(128)}, bf16[128,4096]{1,0:T(8,128)(2,1)}, ...), condition=%wide.region_12.13_spmd.clone, body=%wide.region_2.12_spmd.clone.sunk | while | flops 10228861952 | bytes 284330272 | solution.py:164
  255.1 2.6 fusion.60
  257.8 51.0 %all-gather.6.cloned.1.call-done = bf16[512,4096]{1,0:T(8,128)(2,1)} async-done(((bf16[128,4096]{1,0:T(8,128)(2,1)}), bf16[512,4096]{1,0:T(8,128)(2,1)}) %all-gather.6.cloned.1.call-update) | async-done | bytes 4194320 | tf_op jit(solution)/shard_map/while/body/eval_jaxpr/all_gather | solution.py:93
  308.8 2.1 conditional.6
  311.0 4.2 conditional.7
  311.0 4.2 broadcast.153
  317.1 111.5 %reduce-scatter.5.cloned.1.call-done = f32[128,4096]{1,0:T(8,128)} async-done(((f32[512,4096]{1,0:T(8,128)}), f32[128,4096]{1,0:T(8,128)}) %reduce-scatter.5.cloned.1.call-update) | async-done | bytes 2097168 | tf_op jit(solution)/shard_map/while/body/eval_jaxpr/reduce_scatter | solution.py:111
  438.8 2.6 fusion.60
  441.5 52.8 %all-gather.6.cloned.1.call-done = bf16[512,4096]{1,0:T(8,128)(2,1)} async-done(((bf16[128,4096]{1,0:T(8,128)(2,1)}), bf16[512,4096]{1,0:T(8,128)(2,1)}) %all-gather.6.cloned.1.call-update) | async-done | bytes 4194320 | tf_op jit(solution)/shard_map/while/body/eval_jaxpr/all_gather | solution.py:93
  494.3 21.5 %conditional.6 = (bf16[512,512]{0,1:T(8,128)(2,1)}, bf16[512,1536]{0,1:T(8,128)(2,1)}) conditional(s32[]{:T(128)} %convert_element_type.172, () %tuple.86, (s32[1]{0:T(128)}, s32[512]{0:T(512)S(1)}, bf16[1,512,3,512]{1,3,2,0:T(8,128)(2,1)}, bf16[512,4096]{1,0:T(8,128)(2,1)}, bf16[512,4096]{1,0:T(8,128)(2,1)}) %tuple.87), branch_computations={%region_3.3_spmd, %region_4.6_spmd} | conditional | flops 3773561856 | bytes 103853256 | solution.py:110
  495.0 2.6 fusion.35
  497.6 4.8 fusion.36
  502.4 3.0 fusion.7
  507.5 3.6 fusion.11
  515.8 12.2 %conditional.7 = (f32[512,4096]{1,0:T(8,128)}) conditional(s32[]{:T(128)} %convert_element_type.172, () %tuple.85, (bf16[512,1536]{0,1:T(8,128)(2,1)}, bf16[4096,1536]{1,0:T(8,128)(2,1)}) %tuple.88), branch_computations={%region_7.7_spmd, %region_8.8_spmd} | conditional | flops 6442450944 | bytes 22544392 | solution.py:112
  515.8 12.2 %fusion.37 = f32[512,4096]{1,0:T(8,128)} fusion(bf16[512,1536]{0,1:T(8,128)(2,1)} %get-tuple-element.422, bf16[4096,1536]{1,0:T(8,128)(2,1)} %get-tuple-element.358), kind=kOutput, calls=%fused_computation.65 | convolution fusion | flops 6442450944 | bytes 22544384 | tf_op jit(solution)/shard_map/while/body/eval_jaxpr/cond/branch_1_fun/dot_general | solution.py:114
  530.2 84.5 %reduce-scatter.5.cloned.1.call-done = f32[128,4096]{1,0:T(8,128)} async-done(((f32[512,4096]{1,0:T(8,128)}), f32[128,4096]{1,0:T(8,128)}) %reduce-scatter.5.cloned.1.call-update) | async-done | bytes 2097168 | tf_op jit(solution)/shard_map/while/body/eval_jaxpr/reduce_scatter | solution.py:111
  624.7 7.9 %fusion.26 = f32[512,4096]{1,0:T(8,128)} fusion(bf16[1,512,4096]{2,1,0:T(8,128)(2,1)} %get-tuple-element.385, bf16[1,512,512]{1,2,0:T(8,128)(2,1)} %get-tuple-element.384), kind=kOutput, calls=%fused_computation.48 | convolution fusion | flops 2147483648 | bytes 13107200 | tf_op jit(solution)/shard_map/dot_general | solution.py:22
  632.7 144.6 %reduce-scatter.3.cloned.1.call-done = f32[512,1024]{1,0:T(8,128)} async-done(((f32[512,4096]{1,0:T(8,128)}), f32[512,1024]{1,0:T(8,128)}) %reduce-scatter.3.cloned.1.call-update) | async-done | bytes 2097168 | tf_op jit(solution)/shard_map/reduce_scatter | solution.py:172
  777.3 2.7 convert_bitcast_fusion.1
  (103 shorter events, 42.7 us)
Async XLA Ops:
  7.2 225.8 %all-gather.4.cloned.1.call-start = ((), (), s32[]{:S(2)}) async-start(), calls=%async_computation.3 | async-start | bytes 15728640 | tf_op jit(solution)/shard_map/all_gather | solution.py:73
  11.9 3.0 copy-start.13
  252.6 2.5 copy-start.17
  255.1 53.8 %all-gather.6.cloned.1.call-start = ((), (), s32[]{:S(2)}) async-start(), calls=%async_computation.4 | async-start | bytes 5242880 | tf_op jit(solution)/shard_map/while/body/eval_jaxpr/all_gather | solution.py:93
  257.8 170.9 %reduce-scatter.5.cloned.1.call-start = ((), (), s32[]{:S(2)}) async-start(), calls=%async_computation.5 | async-start | bytes 10485760 | tf_op jit(solution)/shard_map/while/body/eval_jaxpr/reduce_scatter | solution.py:111
  428.7 2.5 copy-start.3
  428.7 2.8 copy-start.11
  431.5 2.7 copy-start.1
  431.5 3.8 copy-start.5
  432.6 3.8 copy-start.12
  432.6 4.8 collective-permute-start
  438.8 55.6 %all-gather.6.cloned.1.call-start = ((), (), s32[]{:S(2)}) async-start(), calls=%async_computation.4 | async-start | bytes 5242880 | tf_op jit(solution)/shard_map/while/body/eval_jaxpr/all_gather | solution.py:93
  441.5 173.2 %reduce-scatter.5.cloned.1.call-start = ((), (), s32[]{:S(2)}) async-start(), calls=%async_computation.5 | async-start | bytes 10485760 | tf_op jit(solution)/shard_map/while/body/eval_jaxpr/reduce_scatter | solution.py:111
  502.4 3.0 copy-start.10
  502.4 4.2 copy-start.6
  502.4 5.1 copy-start.18
  507.5 3.6 copy-start.7
  614.6 2.5 copy-start.3
  614.6 2.8 copy-start.11
  617.4 2.7 copy-start.1
  617.4 3.8 copy-start.5
  618.6 3.8 copy-start.12
  618.6 4.8 collective-permute-start
  624.7 152.6 %reduce-scatter.3.cloned.1.call-start = ((), (), s32[]{:S(2)}) async-start(), calls=%async_computation.2 | async-start | bytes 10485760 | tf_op jit(solution)/shard_map/reduce_scatter | solution.py:172
  (11 other events, 17.3 us)
Sparse Core Ops, SparseCore 0:
  12.0 220.8 all-gather.3
  257.9 50.8 all-gather.5
  315.3 113.2 reduce-scatter.4
  441.6 52.6 all-gather.5
  528.2 86.3 reduce-scatter.4
  632.8 144.4 reduce-scatter.2
where the time goes:
time: 788 us; the launch traced here: 787 us
  waiting for transfers between devices  661 us (84%)
  local copies, waits for them, and re-layouts  46.2 us (6%)
  matrix products  32.7 us (4%)
  other arithmetic  28.4 us (4%)
  between operations  14.9 us (2%)
    all_gather x1, waiting for transfers between devices, body(): weight_rows = lax.all_gather(w_qkv[0], 'dp', axis=0, tiled=True)  215 us
    reduce_scatter x2, waiting for transfers between devices, section_work(): lax.psum_scatter(lax.cond(is_live, lambda start_row: jnp.dot(flat_grads,...  196 us
    reduce_scatter x1, waiting for transfers between devices, body(): lax.psum_scatter(out_local, 'dp', scatter_dimension=1, tiled=True)  145 us
    all_gather x2, waiting for transfers between devices, section_work(): branch_full = lax.all_gather(d_branch, 'seq', axis=0, tiled=True)  104 us
    unnamed x13, local copies, waits for them, and re-layouts  24.3 us
  transfers between devices with their start and end apart: 8, of which 8 were waited for; matrix products, arithmetic and copies ran while one was open for 1% of the time, Pallas kernels for 0%

commit v1 on v0

v1 whole, which is shorter than its diff:
```python
import functools
import math

import jax
import jax.numpy as jnp
from jax import lax
from jax.experimental import pallas as pl
from jax.experimental.pallas import tpu as pltpu
from jax.sharding import PartitionSpec as P

HEAD_DIM = 128
AXES = ("section", "seq", "dp")
F32 = jnp.float32
BF16 = jnp.bfloat16


def dot_nt(left, right):
    return lax.dot_general(left, right, (((1,), (1,)), ((), ())), preferred_element_type=F32)


def dot_nn(left, right):
    return lax.dot_general(left, right, (((1,), (0,)), ((), ())), preferred_element_type=F32)


def dot_tn(left, right):
    return lax.dot_general(left, right, (((0,), (0,)), ((), ())), preferred_element_type=F32)


def d_attn_kernel(info, *refs):
    blocks, w_out, out = refs[:-2], refs[-2], refs[-1]
    rows = blocks[0].shape[0]
    me = info[0]
    for r, block in enumerate(blocks):
        start = pl.multiple_of((me ^ r) * rows, rows)
        out[pl.ds(start, rows), :] = dot_nt(block[...], w_out[...]).astype(BF16)


def d_attn_call(info, blocks, w_out):
    rows, width = blocks[0].shape
    heads_width = w_out.shape[0]
    whole = lambda shape: pl.BlockSpec(shape, lambda step, info: (0, 0))
    count = len(blocks)
    return pl.pallas_call(
        d_attn_kernel,
        out_shape=jax.ShapeDtypeStruct((rows * count, heads_width), BF16),
        grid_spec=pltpu.PrefetchScalarGridSpec(
            num_scalar_prefetch=1,
            grid=(1,),
            in_specs=[whole((rows, width))] * count + [whole(w_out.shape)],
            out_specs=whole((rows * count, heads_width)),
        ),
        compiler_params=pltpu.CompilerParams(vmem_limit_bytes=40 * 1024 * 1024),
        cost_estimate=pl.CostEstimate(
            flops=2 * rows * count * heads_width * width,
            bytes_accessed=2 * (rows * count * width + heads_width * width),
            transcendentals=0,
        ),
    )(info, *blocks, w_out)


def attend_kernel(slot, info, saved, d_attn, weight, attn_rel, *rest):
    outs, (grads, attn_all, partial, w_vmem, w_sem) = rest[:-5], rest[-5:]
    count = len(outs)
    rows = outs[0].shape[0]
    capacity = d_attn.shape[0]
    head = pl.program_id(0)
    head_count = pl.num_programs(0)
    me, live = info[0], info[2 + slot]
    factor = 1.0 / math.sqrt(HEAD_DIM)
    w_copy = pltpu.make_async_copy(weight, w_vmem, w_sem)

    @pl.when(head == 0)
    def _():
        w_copy.start()

    columns = pl.ds(pl.multiple_of(head * HEAD_DIM, HEAD_DIM), HEAD_DIM)

    def one_head(size):
        queries, keys, values = saved[0, :size], saved[1, :size], saved[2, :size]
        upstream = d_attn[:size]
        scores = dot_nt(queries, keys) * factor
        alive = lax.broadcasted_iota(jnp.int32, (1, size), 1) < live
        scores = jnp.where(alive, scores, -1e30)
        weights = jnp.exp(scores - jnp.max(scores, axis=1, keepdims=True))
        weights = weights / jnp.sum(weights, axis=1, keepdims=True)
        rounded = weights.astype(BF16)
        mixed = dot_nn(rounded, values).astype(BF16)
        attn_all[:size, columns] = mixed
        delta = jnp.sum(upstream.astype(F32) * mixed.astype(F32), axis=1, keepdims=True)
        d_scores = (weights * (dot_nt(upstream, values) - delta) * factor).astype(BF16)
        grads[0, :size, columns] = dot_nn(d_scores, keys).astype(BF16)
        grads[1, :size, columns] = dot_tn(d_scores, queries).astype(BF16)
        grads[2, :size, columns] = dot_tn(rounded, upstream).astype(BF16)
        if size < capacity:
            attn_all[size:, columns] = jnp.zeros((capacity - size, HEAD_DIM), BF16)

    half = capacity // 2

    @pl.when(live > half)
    def _():
        one_head(capacity)

    @pl.when(live <= half)
    def _():
        one_head(half)

    @pl.when(head == head_count - 1)
    def _():
        w_copy.wait()
        width = w_vmem.shape[1]
        step = partial.shape[1]

        def project(size):
            for first in range(0, width, step):
                total = dot_nt(grads[0, :size], w_vmem[0, first : first + step])
                total += dot_nt(grads[1, :size], w_vmem[1, first : first + step])
                total += dot_nt(grads[2, :size], w_vmem[2, first : first + step])
                partial[:size] = total
                if size < capacity:
                    partial[size:] = jnp.zeros((capacity - size, step), F32)
                for r in range(count):
                    start = pl.multiple_of((me ^ r) * rows, rows)
                    outs[r][:, first : first + step] = partial[pl.ds(start, rows)].astype(BF16)

        @pl.when(live > half)
        def _():
            project(capacity)

        @pl.when(live <= half)
        def _():
            project(half)

        for r in range(count):
            start = pl.multiple_of((me ^ r) * rows, rows)
            attn_rel[r] = attn_all[pl.ds(start, rows)]


def attend_call(slot, info, saved, d_attn, weight, count):
    capacity, width = d_attn.shape
    rows = capacity // count
    model_cols = weight.shape[1]
    heads = width // HEAD_DIM
    step = min(256, model_cols)
    return pl.pallas_call(
        functools.partial(attend_kernel, slot),
        out_shape=[jax.ShapeDtypeStruct((count, rows, width), BF16)]
        + [jax.ShapeDtypeStruct((rows, model_cols), BF16)] * count,
        grid_spec=pltpu.PrefetchScalarGridSpec(
            num_scalar_prefetch=1,
            grid=(heads,),
            in_specs=[
                pl.BlockSpec((3, capacity, HEAD_DIM), lambda h, info: (0, 0, h)),
                pl.BlockSpec((capacity, HEAD_DIM), lambda h, info: (0, h)),
                pl.BlockSpec(memory_space=pl.ANY),
            ],
            out_specs=[pl.BlockSpec((count, rows, width), lambda h, info: (0, 0, 0))]
            + [pl.BlockSpec((rows, model_cols), lambda h, info: (0, 0))] * count,
            scratch_shapes=[
                pltpu.VMEM((3, capacity, width), BF16),
                pltpu.VMEM((capacity, width), BF16),
                pltpu.VMEM((capacity, step), F32),
                pltpu.VMEM(weight.shape, BF16),
                pltpu.SemaphoreType.DMA,
            ],
        ),
        compiler_params=pltpu.CompilerParams(vmem_limit_bytes=40 * 1024 * 1024),
        cost_estimate=pl.CostEstimate(
            flops=2 * capacity * width * (6 * capacity + 3 * model_cols),
            bytes_accessed=2 * (4 * capacity * width + 3 * model_cols * width + capacity * model_cols),
            transcendentals=capacity * capacity * heads,
        ),
    )(info, saved, d_attn, weight)


def norm_kernel(info, mods, tokens, d_output, *rest):
    blocks, out, d_norm = rest[:-2], rest[-2], rest[-1]
    count = len(blocks)
    width = blocks[0].shape[1]
    for k, block in enumerate(blocks):
        owner = lax.rem(info[1] + (count - k), count)
        start = pl.multiple_of(owner * width, width)
        d_norm[:, pl.ds(start, width)] = block[...].astype(F32)
    values = tokens[...].astype(F32)
    center = values - jnp.mean(values, axis=1, keepdims=True)
    inverse = lax.rsqrt(jnp.mean(center * center, axis=1, keepdims=True) + 1e-06)
    normed = center * inverse
    gained = d_norm[...] * (1.0 + mods[0:1])
    layer = inverse * (
        gained
        - jnp.mean(gained, axis=1, keepdims=True)
        - normed * jnp.mean(gained * normed, axis=1, keepdims=True)
    )
    out[...] = (d_output[...].astype(F32) + layer).astype(BF16)


def norm_call(info, mods, tokens, d_output, blocks):
    rows, width = tokens.shape
    tile = 32
    block_width = blocks[0].shape[1]
    row_spec = lambda cols: pl.BlockSpec((tile, cols), lambda t, info: (t, 0))
    return pl.pallas_call(
        norm_kernel,
        out_shape=jax.ShapeDtypeStruct((rows, width), BF16),
        grid_spec=pltpu.PrefetchScalarGridSpec(
            num_scalar_prefetch=1,
            grid=(rows // tile,),
            in_specs=[pl.BlockSpec(mods.shape, lambda t, info: (0, 0)), row_spec(width), row_spec(width)]
            + [row_spec(block_width)] * len(blocks),
            out_specs=row_spec(width),
            scratch_shapes=[pltpu.VMEM((tile, width), F32)],
        ),
        compiler_params=pltpu.CompilerParams(vmem_limit_bytes=32 * 1024 * 1024),
        cost_estimate=pl.CostEstimate(
            flops=20 * rows * width, bytes_accessed=8 * rows * width, transcendentals=0
        ),
    )(info, mods, tokens, d_output, *blocks)


def body(section_input, saved_qkv, modulation, w_qkv, w_out, lengths, student_out, teacher_target):
    section_total = lax.axis_size("section")
    seq_total = lax.axis_size("seq")
    dp_total = lax.axis_size("dp")
    section_pos = lax.axis_index("section")
    seq_pos = lax.axis_index("seq")
    dp_pos = lax.axis_index("dp")
    tokens = section_input[0, 0]
    mods = modulation[0, 0]
    shard_rows, model_width = tokens.shape
    block_cols = model_width // dp_total
    saved = saved_qkv[0, 0].transpose(1, 0, 2)
    weight = w_qkv[0].transpose(1, 0, 2)
    weight_out = w_out[0]

    def flat(section, seq, dp):
        return (section * seq_total + seq) * dp_total + dp

    def over_dp(value, steps, sections):
        pairs = [
            (flat(s, i, j), flat(s, i, (j + steps) % dp_total))
            for s in sections
            for i in range(seq_total)
            for j in range(dp_total)
        ]
        return lax.ppermute(value, AXES, pairs)

    def over_seq(value, distance, sections):
        pairs = [
            (flat(s, i, j), flat(s, i ^ distance, j))
            for s in sections
            for i in range(seq_total)
            for j in range(dp_total)
        ]
        return lax.ppermute(value, AXES, pairs)

    every = range(section_total)
    live_counts = [lengths] + [over_dp(lengths, -k, every) for k in range(1, dp_total)]
    info = jnp.concatenate([jnp.stack([seq_pos, dp_pos]).astype(jnp.int32)] + live_counts)

    positions = seq_pos * shard_rows + jnp.arange(shard_rows, dtype=jnp.int32)
    gap = student_out[0].astype(F32) - teacher_target[0].astype(F32)
    loss_grad = jnp.where((positions < lengths[0])[:, None], gap, 0.0).astype(BF16)

    def gather_saved(section):
        return [saved] + [over_dp(saved, -k, [section]) for k in range(1, dp_total)]

    def run_section(section, d_output, saved_slots):
        only = [section]
        d_branch = (mods[1] * d_output.astype(F32)).astype(BF16)
        branch_rows = [d_branch] + [over_seq(d_branch, r, only) for r in range(1, seq_total)]
        d_attn = d_attn_call(info, branch_rows, weight_out)
        d_attn_slots = [d_attn] + [over_dp(d_attn, -k, only) for k in range(1, dp_total)]
        attn_slots, home = [], []
        for k in range(dp_total):
            attn_rel, *parts = attend_call(
                k, info, saved_slots[k], d_attn_slots[k], weight, seq_total
            )
            attn_slots.append(attn_rel)
            total = parts[0].astype(F32)
            for r in range(1, seq_total):
                total = total + over_seq(parts[r], r, only).astype(F32)
            total = total.astype(BF16)
            home.append(total if k == 0 else over_dp(total, k, only))
        d_input = norm_call(info, mods, tokens, d_output, home)
        column_blocks = []
        for k in range(dp_total):
            owner = lax.rem(dp_pos + k, dp_total)
            block = lax.dynamic_slice_in_dim(d_branch, owner * block_cols, block_cols, 1)
            column_blocks.append(block if k == 0 else over_dp(block, k, only))
        ordered = [column_blocks[(dp_total - k) % dp_total] for k in range(dp_total)]
        columns = jnp.stack(ordered)
        column_rows = [columns] + [over_seq(columns, r, only) for r in range(1, seq_total)]
        branch_all = jnp.stack(column_rows, axis=1).reshape(-1, block_cols)
        attn_all = jnp.stack(attn_slots).reshape(branch_all.shape[0], -1)
        d_out = dot_tn(attn_all, branch_all).astype(BF16)
        return d_input, d_out

    saved_slots = [gather_saved(section) for section in range(section_total)]
    d_output = loss_grad
    grad_in, grad_out = None, None
    for section in reversed(range(section_total)):
        d_input, d_out = run_section(section, d_output, saved_slots[section])
        if grad_in is None:
            grad_in, grad_out = d_input, d_out
        else:
            grad_in = jnp.where(section_pos == section, d_input, grad_in)
            grad_out = jnp.where(section_pos == section, d_out, grad_out)
        if section > 0:
            pairs = [
                (flat(section, i, j), flat(section - 1, i, j))
                for i in range(seq_total)
                for j in range(dp_total)
            ]
            d_output = lax.ppermute(d_input, AXES, pairs)
    return grad_in[None, None], grad_out[None]


def solution(mesh):
    in_specs = (
        P("section", "dp", "seq", None),
        P("section", "dp", None, None, "seq"),
        P("section", "dp", None, None),
        P("section", "dp", None, "seq"),
        P("section", "seq", None),
        P("dp"),
        P("dp", "seq", None),
        P("dp", "seq", None),
    )
    out_specs = (P("section", "dp", "seq", None), P("section", "seq", "dp"))
    return jax.shard_map(body, mesh=mesh, in_specs=in_specs, out_specs=out_specs, check_vma=False)
```

time: 788 us -> 455 us (0.58); the launches traced: 787 us -> 446 us
  waiting for transfers between devices: 661 us -> 176 us
  starting transfers between devices: 3.24 us -> 155 us
  Pallas kernels: 0 us -> 88.8 us
  local copies, waits for them, and re-layouts: 46.2 us -> 7.39 us
  matrix products: 32.7 us -> 7.32 us
  other arithmetic: 28.4 us -> 7.48 us
  between operations: 14.9 us -> 3.04 us
    reduce_scatter x3 -> x0, waiting for transfers between devices: 341 us -> none  [the longest x2 196 us: section_work(): lax.psum_scatter(lax.cond(is_live, lambda start_row: jnp.dot(flat_grads,...]
    all_gather x3 -> x0, waiting for transfers between devices: 318 us -> none  [the longest x1 215 us: body(): weight_rows = lax.all_gather(w_qkv[0], 'dp', axis=0, tiled=True)]
    ppermute x2 -> x64, waiting for transfers between devices: 2.08 us -> 176 us  [the longest x1 101 us: body(): d_output = lax.ppermute(d_input, AXES, pairs)]
    ppermute x2 -> x64, starting transfers between devices: 3.11 us -> 155 us  [the longest x27 81.5 us: over_dp(): return lax.ppermute(value, AXES, pairs)]
    pallas_call x0 -> x12, Pallas kernels: none -> 88.8 us  [the longest x8 68.2 us: attend_call(): pl.pallas_call(functools.partial(attend_kernel, slot), out_shape=[jax.Sha...]
    dot_general x8 -> x2, matrix products: 27.9 us -> 7.32 us  [dot_tn(): lax.dot_general(left, right, (((0,), (0,)), ((), ())), preferred_element_...]
    unnamed x13 -> x36, local copies, waits for them, and re-layouts: 24.3 us -> 4.57 us
    broadcast_in_dim x7 -> x1, other arithmetic: 11.2 us -> 1.11 us  [body(): return (grad_in[None, None], grad_out[None])]
  transfers between devices with their start and end apart: 8 -> 64, of which waited for: 8 -> 13; matrix products, arithmetic and copies ran while one was open for 1% -> 3% of each run, Pallas kernels for 0% -> 18%
where the time goes in v1:
time: 455 us; the launch traced here: 446 us
  waiting for transfers between devices  176 us (39%)
  starting transfers between devices  155 us (34%)
  Pallas kernels  88.8 us (20%)
  other arithmetic  7.48 us (2%)
  local copies, waits for them, and re-layouts  7.39 us (2%)
  matrix products  7.32 us (2%)
    ppermute x1, waiting for transfers between devices, body(): d_output = lax.ppermute(d_input, AXES, pairs)  101 us
    ppermute x27, starting transfers between devices, over_dp(): return lax.ppermute(value, AXES, pairs)  81.5 us
    ppermute x36, starting transfers between devices, over_seq(): return lax.ppermute(value, AXES, pairs)  72.5 us
    pallas_call x8, Pallas kernels, attend_call(): pl.pallas_call(functools.partial(attend_kernel, slot), out_shape=[jax.Sha...  68.2 us
    ppermute x27, waiting for transfers between devices, over_dp(): return lax.ppermute(value, AXES, pairs)  59.5 us
    ppermute x36, waiting for transfers between devices, over_seq(): return lax.ppermute(value, AXES, pairs)  15.4 us
    pallas_call x2, Pallas kernels, d_attn_call(): pl.pallas_call(d_attn_kernel, out_shape=jax.ShapeDtypeStruct((rows * coun...  14.2 us
  transfers between devices with their start and end apart: 64, of which 13 were waited for; matrix products, arithmetic and copies ran while one was open for 3% of the time, Pallas kernels for 18%

profile of v1, /device:TPU:0, one launch (start us, length us, event | category | flops | bytes accessed | tf_op | source)
XLA Modules:
  0.0 445.5 jit_solution(15429014460175660316)
XLA Ops:
  10.0 5.0 %collective-permute-start = (s32[1]{0:T(128)}, s32[1]{0:T(128)}, u32[]{:S(2)}, u32[]{:S(2)}) collective-permute-start(s32[1]{0:T(128)} %param.13), channel_id=1, source_target_pairs={{0,3},{1,0},{2,1},{3,2},{4,7},{5,4},{6,5},{7,6},{8,11},{9,8},{10,9... | collective-permute-start | bytes 20 | tf_op jit(solution)/shard_map/ppermute | solution.py:244
  34.8 8.0 %shard_map.95.d_attn = bf16[512,512]{1,0:T(8,128)(2,1)S(1)} custom-call(s32[6]{0:T(128)S(1)} %concatenate.3.info, bf16[128,4096]{1,0:T(8,128)(2,1)S(1)} %get-tuple-element.82.refs_0_, bf16[128,4096]{1,0:T(8,128)(2,1)S(1)} %collective-permute-done.3.refs_1_, bf16[128,4096]{1,0:T(8,128)(2,1)} %collective-permute-done.4.refs_2_, ...), custom_call_target="tpu_custom_call" | custom-call | flops 2147483648 | bytes 8388608 | tf_op jit(solution)/shard_map/pallas_call | solution.py:43
  44.3 6.8 %shard_map.96 = (bf16[4,128,512]{2,1,0:T(8,128)(2,1)S(1)}, bf16[128,1024]{1,0:T(8,128)(2,1)S(1)}, bf16[128,1024]{1,0:T(8,128)(2,1)S(1)}, bf16[128,1024]{1,0:T(8,128)(2,1)S(1)}, bf16[128,1024]{1,0:T(8,128)(2,1)S(1)}) custom-call(s32[6]{0:T(128)S(1)} %concatenate.3.info, bf16[3,512,512]{2,1,0:T(8,128)(2,1)} %bitcast.7.saved, ...), custom_call_target="tpu_custom_call" | custom-call | flops 3221225472 | bytes 6291456 | tf_op jit(solution)/shard_map/pallas_call | solution.py:144
  53.1 10.3 %shard_map.97 = (bf16[4,128,512]{2,1,0:T(8,128)(2,1)S(1)}, bf16[128,1024]{1,0:T(8,128)(2,1)S(1)}, bf16[128,1024]{1,0:T(8,128)(2,1)S(1)}, bf16[128,1024]{1,0:T(8,128)(2,1)S(1)}, bf16[128,1024]{1,0:T(8,128)(2,1)S(1)}) custom-call(s32[6]{0:T(128)S(1)} %concatenate.3.info, bf16[3,512,512]{2,1,0:T(8,128)(2,1)} %collective-permute-done.9.saved, ...), custom_call_target="tpu_custom_call" | custom-call | flops 3221225472 | bytes 6291456 | tf_op jit(solution)/shard_map/pallas_call | solution.py:144
  65.5 10.3 %shard_map.98 = (bf16[4,128,512]{2,1,0:T(8,128)(2,1)S(1)}, bf16[128,1024]{1,0:T(8,128)(2,1)S(1)}, bf16[128,1024]{1,0:T(8,128)(2,1)S(1)}, bf16[128,1024]{1,0:T(8,128)(2,1)S(1)}, bf16[128,1024]{1,0:T(8,128)(2,1)S(1)}) custom-call(s32[6]{0:T(128)S(1)} %concatenate.3.info, bf16[3,512,512]{2,1,0:T(8,128)(2,1)} %collective-permute-done.15.saved, ...), custom_call_target="tpu_custom_call" | custom-call | flops 3221225472 | bytes 6291456 | tf_op jit(solution)/shard_map/pallas_call | solution.py:144
  78.8 6.8 %shard_map.99 = (bf16[4,128,512]{2,1,0:T(8,128)(2,1)S(1)}, bf16[128,1024]{1,0:T(8,128)(2,1)S(1)}, bf16[128,1024]{1,0:T(8,128)(2,1)S(1)}, bf16[128,1024]{1,0:T(8,128)(2,1)S(1)}, bf16[128,1024]{1,0:T(8,128)(2,1)S(1)}) custom-call(s32[6]{0:T(128)S(1)} %concatenate.3.info, bf16[3,512,512]{2,1,0:T(8,128)(2,1)} %collective-permute-done.21.saved, ...), custom_call_target="tpu_custom_call" | custom-call | flops 3221225472 | bytes 6291456 | tf_op jit(solution)/shard_map/pallas_call | solution.py:144
  103.9 101.4 %collective-permute-done.27.d_output = bf16[128,4096]{1,0:T(8,128)(2,1)S(1)} collective-permute-done((bf16[128,4096]{1,0:T(8,128)(2,1)}, bf16[128,4096]{1,0:T(8,128)(2,1)S(1)}, u32[]{:S(2)}, u32[]{:S(2)}) %collective-permute-start.27) | collective-permute-done | bytes 1048608 | tf_op jit(solution)/shard_map/ppermute | solution.py:313
  220.7 17.2 %collective-permute-done.54 = bf16[128,1024]{1,0:T(8,128)(2,1)S(1)} collective-permute-done((bf16[128,1024]{1,0:T(8,128)(2,1)S(1)}, bf16[128,1024]{1,0:T(8,128)(2,1)S(1)}, u32[]{:S(2)}, u32[]{:S(2)}) %collective-permute-start.54) | collective-permute-done | bytes 262176 | tf_op jit(solution)/shard_map/ppermute | solution.py:244
  237.9 5.2 %collective-permute-start.53 = (bf16[128,1024]{1,0:T(8,128)(2,1)S(1)}, bf16[128,1024]{1,0:T(8,128)(2,1)S(1)}, u32[]{:S(2)}, u32[]{:S(2)}) collective-permute-start(bf16[128,1024]{1,0:T(8,128)(2,1)S(1)} %get-tuple-element.88), channel_id=1, source_target_pairs={{0,2},{1,3},{2,0},{3,1},{4,6},{5,7},{6,4},{7,5},{8,10},{9,11},{10,... | collective-permute-start | bytes 786440 | tf_op jit(solution)/shard_map/ppermute | solution.py:244
  243.1 7.1 %collective-permute-done.53 = bf16[128,1024]{1,0:T(8,128)(2,1)S(1)} collective-permute-done((bf16[128,1024]{1,0:T(8,128)(2,1)S(1)}, bf16[128,1024]{1,0:T(8,128)(2,1)S(1)}, u32[]{:S(2)}, u32[]{:S(2)}) %collective-permute-start.53) | collective-permute-done | bytes 262176 | tf_op jit(solution)/shard_map/ppermute | solution.py:244
  252.4 6.0 %collective-permute-start.46 = (bf16[3,512,512]{2,1,0:T(8,128)(2,1)}, bf16[3,512,512]{2,1,0:T(8,128)(2,1)}, u32[]{:S(2)}, u32[]{:S(2)}) collective-permute-start(bf16[3,512,512]{2,1,0:T(8,128)(2,1)} %bitcast.7.saved), channel_id=1, source_target_pairs={{0,1},{1,2},{2,3},{3,0},{4,5},{5,6},{6,7},{7,4},{8,9},{9,10},{10,1... | collective-permute-start | bytes 4718600 | tf_op jit(solution)/shard_map/ppermute | solution.py:244
  262.2 6.2 %shard_map.101.d_attn = bf16[512,512]{1,0:T(8,128)(2,1)S(1)} custom-call(s32[6]{0:T(128)S(1)} %concatenate.3.info, bf16[128,4096]{1,0:T(8,128)(2,1)S(1)} %multiply_convert_fusion.refs_0_, bf16[128,4096]{1,0:T(8,128)(2,1)S(1)} %collective-permute-done.28.refs_1_, bf16[128,4096]{1,0:T(8,128)(2,1)S(1)} %collective-permute-done.29.refs_2_, ...), custom_call_target="tpu_custom_call" | custom-call | flops 2147483648 | bytes 8388608 | tf_op jit(solution)/shard_map/pallas_call | solution.py:43
  268.4 21.9 %collective-permute-done.52 = bf16[128,1024]{1,0:T(8,128)(2,1)S(1)} collective-permute-done((bf16[128,1024]{1,0:T(8,128)(2,1)S(1)}, bf16[128,1024]{1,0:T(8,128)(2,1)S(1)}, u32[]{:S(2)}, u32[]{:S(2)}) %collective-permute-start.52) | collective-permute-done | bytes 262176 | tf_op jit(solution)/shard_map/ppermute | solution.py:244
  291.0 6.5 %collective-permute-start.35 = (bf16[512,512]{1,0:T(8,128)(2,1)S(1)}, bf16[512,512]{1,0:T(8,128)(2,1)}, u32[]{:S(2)}, u32[]{:S(2)}) collective-permute-start(bf16[512,512]{1,0:T(8,128)(2,1)S(1)} %shard_map.101.d_attn), channel_id=1, source_target_pairs={{0,3},{1,0},{2,1},{3,2},{4,7},{5,4},{6,5},{7,6},{8,11},{9,8},{10,9... | collective-permute-start | bytes 1572872 | tf_op jit(solution)/shard_map/ppermute | solution.py:244
  298.8 19.5 %collective-permute-start.41 = (bf16[512,512]{1,0:T(8,128)(2,1)S(1)}, bf16[512,512]{1,0:T(8,128)(2,1)S(1)}, u32[]{:S(2)}, u32[]{:S(2)}) collective-permute-start(bf16[512,512]{1,0:T(8,128)(2,1)S(1)} %shard_map.101.d_attn), channel_id=1, source_target_pairs={{0,2},{1,3},{2,0},{3,1},{4,6},{5,7},{6,4},{7,5},{8,10},{9,11},{10,... | collective-permute-start | bytes 1572872 | tf_op jit(solution)/shard_map/ppermute | solution.py:244
  318.3 6.8 %shard_map.102 = (bf16[4,128,512]{2,1,0:T(8,128)(2,1)S(1)}, bf16[128,1024]{1,0:T(8,128)(2,1)S(1)}, bf16[128,1024]{1,0:T(8,128)(2,1)S(1)}, bf16[128,1024]{1,0:T(8,128)(2,1)S(1)}, bf16[128,1024]{1,0:T(8,128)(2,1)S(1)}) custom-call(s32[6]{0:T(128)S(1)} %concatenate.3.info, bf16[3,512,512]{2,1,0:T(8,128)(2,1)} %bitcast.7.saved, ...), custom_call_target="tpu_custom_call" | custom-call | flops 3221225472 | bytes 6291456 | tf_op jit(solution)/shard_map/pallas_call | solution.py:144
  325.1 5.1 %collective-permute-start.47 = (bf16[512,512]{1,0:T(8,128)(2,1)S(1)}, bf16[512,512]{1,0:T(8,128)(2,1)S(1)}, u32[]{:S(2)}, u32[]{:S(2)}) collective-permute-start(bf16[512,512]{1,0:T(8,128)(2,1)S(1)} %shard_map.101.d_attn), channel_id=1, source_target_pairs={{0,1},{1,2},{2,3},{3,0},{4,5},{5,6},{6,7},{7,4},{8,9},{9,10},{10,1... | collective-permute-start | bytes 1572872 | tf_op jit(solution)/shard_map/ppermute | solution.py:244
  330.2 10.3 %shard_map.103 = (bf16[4,128,512]{2,1,0:T(8,128)(2,1)S(1)}, bf16[128,1024]{1,0:T(8,128)(2,1)S(1)}, bf16[128,1024]{1,0:T(8,128)(2,1)S(1)}, bf16[128,1024]{1,0:T(8,128)(2,1)S(1)}, bf16[128,1024]{1,0:T(8,128)(2,1)S(1)}) custom-call(s32[6]{0:T(128)S(1)} %concatenate.3.info, bf16[3,512,512]{2,1,0:T(8,128)(2,1)} %collective-permute-done.34.saved, ...), custom_call_target="tpu_custom_call" | custom-call | flops 3221225472 | bytes 6291456 | tf_op jit(solution)/shard_map/pallas_call | solution.py:144
  340.5 4.4 collective-permute-start.33
  350.0 10.3 %shard_map.104 = (bf16[4,128,512]{2,1,0:T(8,128)(2,1)S(1)}, bf16[128,1024]{1,0:T(8,128)(2,1)S(1)}, bf16[128,1024]{1,0:T(8,128)(2,1)S(1)}, bf16[128,1024]{1,0:T(8,128)(2,1)S(1)}, bf16[128,1024]{1,0:T(8,128)(2,1)S(1)}) custom-call(s32[6]{0:T(128)S(1)} %concatenate.3.info, bf16[3,512,512]{2,1,0:T(8,128)(2,1)} %collective-permute-done.40.saved, ...), custom_call_target="tpu_custom_call" | custom-call | flops 3221225472 | bytes 6291456 | tf_op jit(solution)/shard_map/pallas_call | solution.py:144
  360.3 4.4 collective-permute-start.38
  376.7 6.8 %shard_map.105 = (bf16[4,128,512]{2,1,0:T(8,128)(2,1)S(1)}, bf16[128,1024]{1,0:T(8,128)(2,1)S(1)}, bf16[128,1024]{1,0:T(8,128)(2,1)S(1)}, bf16[128,1024]{1,0:T(8,128)(2,1)S(1)}, bf16[128,1024]{1,0:T(8,128)(2,1)S(1)}) custom-call(s32[6]{0:T(128)S(1)} %concatenate.3.info, bf16[3,512,512]{2,1,0:T(8,128)(2,1)} %collective-permute-done.46.saved, ...), custom_call_target="tpu_custom_call" | custom-call | flops 3221225472 | bytes 6291456 | tf_op jit(solution)/shard_map/pallas_call | solution.py:144
  403.8 11.4 %collective-permute-done.42 = bf16[128,1024]{1,0:T(8,128)(2,1)S(1)} collective-permute-done((bf16[128,1024]{1,0:T(8,128)(2,1)S(1)}, bf16[128,1024]{1,0:T(8,128)(2,1)S(1)}, u32[]{:S(2)}, u32[]{:S(2)}) %collective-permute-start.42) | collective-permute-done | bytes 262176 | tf_op jit(solution)/shard_map/ppermute | solution.py:253
  429.1 4.5 %collective-permute-start.51 = (bf16[128,1024]{1,0:T(8,128)(2,1)S(1)}, bf16[128,1024]{1,0:T(8,128)(2,1)S(1)}, u32[]{:S(2)}, u32[]{:S(2)}) collective-permute-start(bf16[128,1024]{1,0:T(8,128)(2,1)S(1)} %add_convert_fusion), channel_id=1, source_target_pairs={{0,3},{1,0},{2,1},{3,2},{4,7},{5,4},{6,5},{7,6},{8,11},{9,8},{10,9... | collective-permute-start | bytes 786440 | tf_op jit(solution)/shard_map/ppermute | solution.py:244
  (172 shorter events, 140.5 us)
Async XLA Ops:
  4.1 24.9 %collective-permute-start.3 = (bf16[128,4096]{1,0:T(8,128)(2,1)S(1)}, bf16[128,4096]{1,0:T(8,128)(2,1)S(1)}, u32[]{:S(2)}, u32[]{:S(2)}) collective-permute-start(bf16[128,4096]{1,0:T(8,128)(2,1)S(1)} %get-tuple-element.82.refs_0_), channel_id=1, source_target_pairs={{16,20},{17,21},{18,22},{19,23},{20,16},{21,17},{22,18},{23,19},{2... | collective-permute-start | bytes 3145736 | tf_op jit(solution)/shard_map/ppermute | solution.py:253
  4.9 27.8 %collective-permute-start.4 = (bf16[128,4096]{1,0:T(8,128)(2,1)S(1)}, bf16[128,4096]{1,0:T(8,128)(2,1)}, u32[]{:S(2)}, u32[]{:S(2)}) collective-permute-start(bf16[128,4096]{1,0:T(8,128)(2,1)S(1)} %get-tuple-element.82.refs_0_), channel_id=1, source_target_pairs={{16,24},{17,25},{18,26},{19,27},{20,28},{21,29},{22,30},{23,31},{2... | collective-permute-start | bytes 3145736 | tf_op jit(solution)/shard_map/ppermute | solution.py:253
  6.5 26.1 %collective-permute-start.5 = (bf16[128,4096]{1,0:T(8,128)(2,1)S(1)}, bf16[128,4096]{1,0:T(8,128)(2,1)}, u32[]{:S(2)}, u32[]{:S(2)}) collective-permute-start(bf16[128,4096]{1,0:T(8,128)(2,1)S(1)} %get-tuple-element.82.refs_0_), channel_id=1, source_target_pairs={{16,28},{17,29},{18,30},{19,31},{20,24},{21,25},{22,26},{23,27},{2... | collective-permute-start | bytes 3145736 | tf_op jit(solution)/shard_map/ppermute | solution.py:253
  8.2 44.9 %collective-permute-start.9 = (bf16[3,512,512]{2,1,0:T(8,128)(2,1)}, bf16[3,512,512]{2,1,0:T(8,128)(2,1)}, u32[]{:S(2)}, u32[]{:S(2)}) collective-permute-start(bf16[3,512,512]{2,1,0:T(8,128)(2,1)} %bitcast.7.saved), channel_id=1, source_target_pairs={{16,19},{17,16},{18,17},{19,18},{20,23},{21,20},{22,21},{23,22},{2... | collective-permute-start | bytes 4718600 | tf_op jit(solution)/shard_map/ppermute | solution.py:244
  27.2 37.6 %collective-permute-start.15 = (bf16[3,512,512]{2,1,0:T(8,128)(2,1)}, bf16[3,512,512]{2,1,0:T(8,128)(2,1)}, u32[]{:S(2)}, u32[]{:S(2)}) collective-permute-start(bf16[3,512,512]{2,1,0:T(8,128)(2,1)} %bitcast.7.saved), channel_id=1, source_target_pairs={{16,18},{17,19},{18,16},{19,17},{20,22},{21,23},{22,20},{23,21},{2... | collective-permute-start | bytes 4718600 | tf_op jit(solution)/shard_map/ppermute | solution.py:244
  29.0 48.3 %collective-permute-start.21 = (bf16[3,512,512]{2,1,0:T(8,128)(2,1)}, bf16[3,512,512]{2,1,0:T(8,128)(2,1)}, u32[]{:S(2)}, u32[]{:S(2)}) collective-permute-start(bf16[3,512,512]{2,1,0:T(8,128)(2,1)} %bitcast.7.saved), channel_id=1, source_target_pairs={{16,17},{17,18},{18,19},{19,16},{20,21},{21,22},{22,23},{23,20},{2... | collective-permute-start | bytes 4718600 | tf_op jit(solution)/shard_map/ppermute | solution.py:244
  51.9 24.7 %collective-permute-start.22 = (bf16[512,512]{1,0:T(8,128)(2,1)S(1)}, bf16[512,512]{1,0:T(8,128)(2,1)S(1)}, u32[]{:S(2)}, u32[]{:S(2)}) collective-permute-start(bf16[512,512]{1,0:T(8,128)(2,1)S(1)} %shard_map.95.d_attn), channel_id=1, source_target_pairs={{16,17},{17,18},{18,19},{19,16},{20,21},{21,22},{22,23},{23,20},{2... | collective-permute-start | bytes 1572872 | tf_op jit(solution)/shard_map/ppermute | solution.py:244
  96.4 108.9 %collective-permute-start.27 = (bf16[128,4096]{1,0:T(8,128)(2,1)}, bf16[128,4096]{1,0:T(8,128)(2,1)S(1)}, u32[]{:S(2)}, u32[]{:S(2)}) collective-permute-start(bf16[128,4096]{1,0:T(8,128)(2,1)} %shard_map.100), channel_id=1, source_target_pairs={{16,0},{17,1},{18,2},{19,3},{20,4},{21,5},{22,6},{23,7},{24,8},{25... | collective-permute-start | bytes 3145736 | tf_op jit(solution)/shard_map/ppermute | solution.py:313
  101.4 114.6 %collective-permute-start.63 = (bf16[4,128,1024]{2,1,0:T(8,128)(2,1)}, bf16[4,128,1024]{2,1,0:T(8,128)(2,1)}, u32[]{:S(2)}, u32[]{:S(2)}) collective-permute-start(bf16[4,128,1024]{2,1,0:T(8,128)(2,1)} %get-tuple-element.91), channel_id=1, source_target_pairs={{16,28},{17,29},{18,30},{19,31},{20,24},{21,25},{22,26},{23,27},{2... | collective-permute-start | bytes 3145736 | tf_op jit(solution)/shard_map/ppermute | solution.py:253
  103.2 115.2 %collective-permute-start.62 = (bf16[4,128,1024]{2,1,0:T(8,128)(2,1)}, bf16[4,128,1024]{2,1,0:T(8,128)(2,1)S(1)}, u32[]{:S(2)}, u32[]{:S(2)}) collective-permute-start(bf16[4,128,1024]{2,1,0:T(8,128)(2,1)} %get-tuple-element.91), channel_id=1, source_target_pairs={{16,24},{17,25},{18,26},{19,27},{20,28},{21,29},{22,30},{23,31},{2... | collective-permute-start | bytes 3145736 | tf_op jit(solution)/shard_map/ppermute | solution.py:253
  205.5 46.9 %collective-permute-start.28 = (bf16[128,4096]{1,0:T(8,128)(2,1)S(1)}, bf16[128,4096]{1,0:T(8,128)(2,1)S(1)}, u32[]{:S(2)}, u32[]{:S(2)}) collective-permute-start(bf16[128,4096]{1,0:T(8,128)(2,1)S(1)} %multiply_convert_fusion.refs_0_), channel_id=1, source_target_pairs={{0,4},{1,5},{2,6},{3,7},{4,0},{5,1},{6,2},{7,3},{8,12},{9,13},{10,... | collective-permute-start | bytes 3145736 | tf_op jit(solution)/shard_map/ppermute | solution.py:253
  208.9 89.9 %collective-permute-start.34 = (bf16[3,512,512]{2,1,0:T(8,128)(2,1)}, bf16[3,512,512]{2,1,0:T(8,128)(2,1)}, u32[]{:S(2)}, u32[]{:S(2)}) collective-permute-start(bf16[3,512,512]{2,1,0:T(8,128)(2,1)} %bitcast.7.saved), channel_id=1, source_target_pairs={{0,3},{1,0},{2,1},{3,2},{4,7},{5,4},{6,5},{7,6},{8,11},{9,8},{10,9... | collective-permute-start | bytes 4718600 | tf_op jit(solution)/shard_map/ppermute | solution.py:244
  212.5 45.9 %collective-permute-start.29 = (bf16[128,4096]{1,0:T(8,128)(2,1)S(1)}, bf16[128,4096]{1,0:T(8,128)(2,1)S(1)}, u32[]{:S(2)}, u32[]{:S(2)}) collective-permute-start(bf16[128,4096]{1,0:T(8,128)(2,1)S(1)} %multiply_convert_fusion.refs_0_), channel_id=1, source_target_pairs={{0,8},{1,9},{2,10},{3,11},{4,12},{5,13},{6,14},{7,15},{8,0},{9,1},... | collective-permute-start | bytes 3145736 | tf_op jit(solution)/shard_map/ppermute | solution.py:253
  216.1 44.3 %collective-permute-start.30 = (bf16[128,4096]{1,0:T(8,128)(2,1)S(1)}, bf16[128,4096]{1,0:T(8,128)(2,1)S(1)}, u32[]{:S(2)}, u32[]{:S(2)}) collective-permute-start(bf16[128,4096]{1,0:T(8,128)(2,1)S(1)} %multiply_convert_fusion.refs_0_), channel_id=1, source_target_pairs={{0,12},{1,13},{2,14},{3,15},{4,8},{5,9},{6,10},{7,11},{8,4},{9,5},... | collective-permute-start | bytes 3145736 | tf_op jit(solution)/shard_map/ppermute | solution.py:253
  250.3 94.6 %collective-permute-start.40 = (bf16[3,512,512]{2,1,0:T(8,128)(2,1)}, bf16[3,512,512]{2,1,0:T(8,128)(2,1)}, u32[]{:S(2)}, u32[]{:S(2)}) collective-permute-start(bf16[3,512,512]{2,1,0:T(8,128)(2,1)} %bitcast.7.saved), channel_id=1, source_target_pairs={{0,2},{1,3},{2,0},{3,1},{4,6},{5,7},{6,4},{7,5},{8,10},{9,11},{10,... | collective-permute-start | bytes 4718600 | tf_op jit(solution)/shard_map/ppermute | solution.py:244
  252.4 107.9 %collective-permute-start.46 = (bf16[3,512,512]{2,1,0:T(8,128)(2,1)}, bf16[3,512,512]{2,1,0:T(8,128)(2,1)}, u32[]{:S(2)}, u32[]{:S(2)}) collective-permute-start(bf16[3,512,512]{2,1,0:T(8,128)(2,1)} %bitcast.7.saved), channel_id=1, source_target_pairs={{0,1},{1,2},{2,3},{3,0},{4,5},{5,6},{6,7},{7,4},{8,9},{9,10},{10,1... | collective-permute-start | bytes 4718600 | tf_op jit(solution)/shard_map/ppermute | solution.py:244
  258.5 31.8 %collective-permute-start.52 = (bf16[128,1024]{1,0:T(8,128)(2,1)S(1)}, bf16[128,1024]{1,0:T(8,128)(2,1)S(1)}, u32[]{:S(2)}, u32[]{:S(2)}) collective-permute-start(bf16[128,1024]{1,0:T(8,128)(2,1)S(1)} %get-tuple-element.89), channel_id=1, source_target_pairs={{0,3},{1,0},{2,1},{3,2},{4,7},{5,4},{6,5},{7,6},{8,11},{9,8},{10,9... | collective-permute-start | bytes 786440 | tf_op jit(solution)/shard_map/ppermute | solution.py:244
  260.4 80.1 %collective-permute-start.61 = (bf16[4,128,1024]{2,1,0:T(8,128)(2,1)}, bf16[4,128,1024]{2,1,0:T(8,128)(2,1)}, u32[]{:S(2)}, u32[]{:S(2)}) collective-permute-start(bf16[4,128,1024]{2,1,0:T(8,128)(2,1)} %get-tuple-element.91), channel_id=1, source_target_pairs={{16,20},{17,21},{18,22},{19,23},{20,16},{21,17},{22,18},{23,19},{2... | collective-permute-start | bytes 3145736 | tf_op jit(solution)/shard_map/ppermute | solution.py:253
  291.0 34.1 %collective-permute-start.35 = (bf16[512,512]{1,0:T(8,128)(2,1)S(1)}, bf16[512,512]{1,0:T(8,128)(2,1)}, u32[]{:S(2)}, u32[]{:S(2)}) collective-permute-start(bf16[512,512]{1,0:T(8,128)(2,1)S(1)} %shard_map.101.d_attn), channel_id=1, source_target_pairs={{0,3},{1,0},{2,1},{3,2},{4,7},{5,4},{6,5},{7,6},{8,11},{9,8},{10,9... | collective-permute-start | bytes 1572872 | tf_op jit(solution)/shard_map/ppermute | solution.py:244
  298.8 48.5 %collective-permute-start.41 = (bf16[512,512]{1,0:T(8,128)(2,1)S(1)}, bf16[512,512]{1,0:T(8,128)(2,1)S(1)}, u32[]{:S(2)}, u32[]{:S(2)}) collective-permute-start(bf16[512,512]{1,0:T(8,128)(2,1)S(1)} %shard_map.101.d_attn), channel_id=1, source_target_pairs={{0,2},{1,3},{2,0},{3,1},{4,6},{5,7},{6,4},{7,5},{8,10},{9,11},{10,... | collective-permute-start | bytes 1572872 | tf_op jit(solution)/shard_map/ppermute | solution.py:244
  325.1 48.9 %collective-permute-start.47 = (bf16[512,512]{1,0:T(8,128)(2,1)S(1)}, bf16[512,512]{1,0:T(8,128)(2,1)S(1)}, u32[]{:S(2)}, u32[]{:S(2)}) collective-permute-start(bf16[512,512]{1,0:T(8,128)(2,1)S(1)} %shard_map.101.d_attn), channel_id=1, source_target_pairs={{0,1},{1,2},{2,3},{3,0},{4,5},{5,6},{6,7},{7,4},{8,9},{9,10},{10,1... | collective-permute-start | bytes 1572872 | tf_op jit(solution)/shard_map/ppermute | solution.py:244
  383.5 45.6 %collective-permute-start.57 = (bf16[4,128,1024]{2,1,0:T(8,128)(2,1)S(1)}, bf16[4,128,1024]{2,1,0:T(8,128)(2,1)S(1)}, u32[]{:S(2)}, u32[]{:S(2)}) collective-permute-start(bf16[4,128,1024]{2,1,0:T(8,128)(2,1)S(1)} %get-tuple-element.85), channel_id=1, source_target_pairs={{0,12},{1,13},{2,14},{3,15},{4,8},{5,9},{6,10},{7,11},{8,4},{9,5},... | collective-permute-start | bytes 3145736 | tf_op jit(solution)/shard_map/ppermute | solution.py:253
  386.9 46.6 %collective-permute-start.56 = (bf16[4,128,1024]{2,1,0:T(8,128)(2,1)S(1)}, bf16[4,128,1024]{2,1,0:T(8,128)(2,1)S(1)}, u32[]{:S(2)}, u32[]{:S(2)}) collective-permute-start(bf16[4,128,1024]{2,1,0:T(8,128)(2,1)S(1)} %get-tuple-element.85), channel_id=1, source_target_pairs={{0,8},{1,9},{2,10},{3,11},{4,12},{5,13},{6,14},{7,15},{8,0},{9,1},... | collective-permute-start | bytes 3145736 | tf_op jit(solution)/shard_map/ppermute | solution.py:253
  389.3 44.2 %collective-permute-start.55 = (bf16[4,128,1024]{2,1,0:T(8,128)(2,1)S(1)}, bf16[4,128,1024]{2,1,0:T(8,128)(2,1)S(1)}, u32[]{:S(2)}, u32[]{:S(2)}) collective-permute-start(bf16[4,128,1024]{2,1,0:T(8,128)(2,1)S(1)} %get-tuple-element.85), channel_id=1, source_target_pairs={{0,4},{1,5},{2,6},{3,7},{4,0},{5,1},{6,2},{7,3},{8,12},{9,13},{10,... | collective-permute-start | bytes 3145736 | tf_op jit(solution)/shard_map/ppermute | solution.py:253
  (58 other events, 909.2 us)
